TPU v7x, 256 devices: a whole 4x4x8 slice. The times are simulated.
256 devices in a mesh: row: 16 (over z, core), col: 16 (over y, x).
Axes of the slice: x: 4, y: 4, z: 8, core: 2. Of those that a mesh axis runs over, the one named last changes fastest.
Arguments:
- eigvecs: bfloat16 [98304, 8192], P('row', 'col'), may hold values from -6 to 6
- panels: bfloat16 [2, 128, 98304], P(None, 'col', 'row'), may hold values from -0.078125 to 0.078125
- tfactors: float32 [2, 128, 128], replicated, may hold values from -0.1 to 0.5, as said below
- offsets: int32 [2], replicated, may hold values from 0 to 98176
Outputs:
- result: bfloat16 [98304, 8192], P('row', 'col')
Inputs may be any that keep to these rules, and one draw needn't show every extreme that they name: Entries below the diagonal of each tfactors[p] are zero.
All inputs are finite; a program needn't handle non-finite values.
Results may differ from a plain program's by a relative error of at most 0.0034.
Values may be sent and summed in bfloat16 or wider, within the bound.
A program may use at most 64 MiB of HBM per device.

v0:
```python
import jax
import jax.numpy as jnp
from jax import lax
from jax.sharding import PartitionSpec as P


def local(eigvecs, panels, tfactors, offsets):
    whole = lax.all_gather(panels, "col", axis=1, tiled=True)
    width = whole.shape[1]
    rows = whole.shape[2]
    start = lax.axis_index("row") * rows
    position = start + lax.broadcasted_iota(jnp.int32, (width, rows), 1)
    column = lax.broadcasted_iota(jnp.int32, (width, rows), 0)

    def reflector(p):
        pivot = offsets[p] + column
        unit = jnp.where(position == pivot, 1.0, 0.0).astype(jnp.bfloat16)
        return jnp.where(position > pivot, whole[p], unit)

    first = reflector(0)
    second = reflector(1)
    upper = jnp.triu(tfactors)
    high = lax.Precision.HIGHEST
    dims = (((0,), (0,)), ((), ()))
    local_cross = lax.dot_general(
        first, second, (((1,), (1,)), ((), ())), preferred_element_type=jnp.float32
    )
    local_zero = jnp.dot(first, eigvecs, preferred_element_type=jnp.float32)
    local_one = jnp.dot(second, eigvecs, preferred_element_type=jnp.float32)
    coeff_one = lax.psum(local_one, "row")
    shift_one = jnp.dot(upper[1], coeff_one, precision=high).astype(jnp.bfloat16)
    term_zero = local_zero - jnp.dot(local_cross, shift_one.astype(jnp.float32), precision=high)
    coeff_zero = lax.psum(term_zero, "row")
    shift_zero = jnp.dot(upper[0], coeff_zero, precision=high).astype(jnp.bfloat16)
    stacked = jnp.concatenate([second, first], axis=0)
    shifts = jnp.concatenate([shift_one, shift_zero], axis=0)
    final = eigvecs.astype(jnp.float32) - lax.dot_general(
        stacked, shifts, dims, preferred_element_type=jnp.float32
    )
    return final.astype(jnp.bfloat16)


def solution(mesh):
    return jax.shard_map(
        local,
        mesh=mesh,
        in_specs=(P("row", "col"), P(None, "col", "row"), P(), P()),
        out_specs=P("row", "col"),
        check_vma=False,
    )
```

profile of v0, /device:TPU:1, one launch (start us, length us, event | category | flops | bytes accessed | tf_op | source)
XLA Modules:
  0.0 305.9 jit_solution(6206784573288020102)
XLA Ops:
  6.5 0.0 all-gather.2.cloned.1.call-start
  6.5 0.7 all-gather.2.cloned.1.call-update
  7.3 0.0 all-reduce.3.cloned.1.call-start
  7.3 1.3 fusion.21
  8.6 1.3 iota_add_fusion.2
  9.9 0.1 iota_compare_fusion
  10.0 0.9 broadcast_select_fusion
  11.0 55.3 %all-gather.2.cloned.1.call-done = bf16[2,128,6144]{2,1,0:T(8,128)(2,1)} async-done(((bf16[2,8,6144]{2,1,0:T(8,128)(2,1)}), bf16[2,128,6144]{2,1,0:T(8,128)(2,1)}) %all-gather.2.cloned.1.call-update) | async-done | bytes 3145744 | tf_op jit(solution)/shard_map/all_gather | solution.py:8
  66.3 0.0 copy-start
  66.3 3.2 %compare_select_fusion.3 = (bf16[128,6144]{1,0:T(8,128)(2,1)S(1)}, bf16[128,6144]{1,0:T(8,128)(2,1)S(1)}) fusion(s32[6144]{0:T(1024)S(1)} %iota_add_fusion, s32[128]{0:T(128)S(1)} %get-tuple-element.10, bf16[2,128,6144]{2,1,0:T(8,128)(2,1)} %all-gather.2.cloned.1.call-done, s32[128]{0:T(128)S(1)} %get-tuple-element.9), kind=kLoop, calls=%fused_computation.11 | loop fusion | flops 7864320 | bytes 6317056 | tf_op jit(solution)/shard_map/jit(_where)/select_n | solution.py:18
  69.5 0.5 copy-done
  70.0 1.7 fusion.22
  71.7 0.0 all-reduce.3.cloned.1.call-update
  71.7 0.0 all-reduce.5.cloned.1.call-start
  71.8 3.8 %fusion.4 = f32[128,128]{1,0:T(8,128)} fusion(s32[6144]{0:T(1024)S(1)} %iota_add_fusion, s32[128]{0:T(128)S(1)} %get-tuple-element.10, s32[128]{0:T(128)S(1)} %get-tuple-element.9, bf16[2,128,6144]{2,1,0:T(8,128)(2,1)} %all-gather.2.cloned.1.call-done), kind=kOutput, calls=%fused_computation.13 | convolution fusion | flops 209190912 | bytes 3261440 | tf_op jit(solution)/shard_map/dot_general | solution.py:25
  75.6 3.8 %fusion.23 = f32[128,512]{1,0:T(8,128)S(1)} fusion(bf16[128,6144]{1,0:T(8,128)(2,1)S(1)} %get-tuple-element.6, bf16[6144,512]{1,0:T(8,128)(2,1)} %param.4), kind=kOutput, calls=%fused_computation.41 | convolution fusion | flops 805306368 | bytes 8126464 | tf_op jit(solution)/shard_map/dot_general | solution.py:28
  79.4 100.3 %all-reduce.3.cloned.1.call-done = f32[128,512]{1,0:T(8,128)} async-done(((f32[128,512]{1,0:T(8,128)}), f32[128,512]{1,0:T(8,128)}) %all-reduce.3.cloned.1.call-update) | async-done | bytes 262160 | tf_op jit(solution)/shard_map/psum | solution.py:30
  179.6 1.3 convolution_convert_fusion.1
  181.0 0.0 copy-start.1
  181.0 0.6 copy-done.1
  181.6 1.8 convolution_subtract_fusion
  183.4 0.0 all-reduce.5.cloned.1.call-update
  183.4 109.0 %all-reduce.5.cloned.1.call-done = f32[128,512]{1,0:T(8,128)} async-done(((f32[128,512]{1,0:T(8,128)}), f32[128,512]{1,0:T(8,128)}) %all-reduce.5.cloned.1.call-update) | async-done | bytes 262160 | tf_op jit(solution)/shard_map/psum | solution.py:33
  292.5 1.3 convolution_convert_fusion
  293.8 5.6 %subtract_convert_fusion = bf16[6144,512]{1,0:T(8,128)(2,1)} fusion(bf16[6144,512]{1,0:T(8,128)(2,1)} %param.4, bf16[128,6144]{1,0:T(8,128)(2,1)S(1)} %get-tuple-element.6, bf16[128,6144]{1,0:T(8,128)(2,1)S(1)} %get-tuple-element.5, bf16[128,512]{1,0:T(8,128)(2,1)S(1)} %convolution_convert_fusion, bf16[128,512]{1,0:T(8,128)(2,1)} %copy-done.1), kind=kOutput, calls=%fused_computation | convolution fusion | flops 1626865664 | bytes 15990784 | tf_op jit(solution)/shard_map/dot_general | solution.py:37
  (2 shorter events, 0.0 us)
Async XLA Ops:
  6.5 59.7 %all-gather.2.cloned.1.call-start = ((), (), s32[]{:S(2)}) async-start(), calls=%async_computation | async-start | bytes 3342336 | tf_op jit(solution)/shard_map/all_gather | solution.py:8
  7.3 172.4 %all-reduce.3.cloned.1.call-start = ((), (), s32[]{:S(2)}) async-start(), calls=%async_computation.1 | async-start | bytes 524288 | tf_op jit(solution)/shard_map/psum | solution.py:30
  66.3 3.7 %copy-start = (bf16[6144,512]{1,0:T(8,128)(2,1)S(1)}, bf16[6144,512]{1,0:T(8,128)(2,1)}, u32[]{:S(2)}) copy-start(bf16[6144,512]{1,0:T(8,128)(2,1)} %param.4) | copy-start | bytes 18874372
  71.7 220.7 %all-reduce.5.cloned.1.call-start = ((), (), s32[]{:S(2)}) async-start(), calls=%async_computation.2 | async-start | bytes 524288 | tf_op jit(solution)/shard_map/psum | solution.py:33
  181.0 0.6 copy-start.1
Sparse Core Ops, SparseCore 0:
  9.8 56.4 all-gather.1
  71.8 107.7 all-reduce.2
  183.6 108.8 all-reduce.4
where the time goes:
time: 306 us
  waiting for transfers between devices  265 us (87%)
  matrix products  19.3 us (6%)
  between operations  13.2 us (4%)
  other arithmetic  5.52 us (2%)
    psum x1, waiting for transfers between devices, local(): coeff_zero = lax.psum(term_zero, 'row')  109 us
    psum x1, waiting for transfers between devices, local(): coeff_one = lax.psum(local_one, 'row')  100 us
    all_gather x1, waiting for transfers between devices, local(): whole = lax.all_gather(panels, 'col', axis=1, tiled=True)  55.3 us
  transfers between devices with their start and end apart: 3, of which 3 were waited for; matrix products, arithmetic and copies ran while one was open for 4% of the time, Pallas kernels for 0%

commit v1 on v0

v1 whole, which is shorter than its diff:
```python
import jax
import jax.numpy as jnp
from jax import lax
from jax.experimental import pallas as pl
from jax.experimental.pallas import tpu as pltpu
from jax.sharding import PartitionSpec as P

MESH = pl.DeviceIdType.MESH
F32 = jnp.float32
BF16 = jnp.bfloat16
HIGH = lax.Precision.HIGHEST

NB = 128
RD = 6144
KD = 512
NX = 4
NZ = 8
OWN = 16
Q = 2 * NB
HALF = RD // 2
QUART = RD // 4
CHUNK = NX * OWN
KT = 1536
ORDER = (0, 1, 3, 2)


def expand(a, panel):
    zero = jnp.zeros((8, a.shape[1]), a.dtype)
    rows = []
    for sx in range(NX):
        for sy in range(NX):
            o = (sy * NX + sx) * 8
            pair = [zero, zero]
            pair[panel] = a[o : o + 8, :]
            rows += pair
    return jnp.concatenate(rows, axis=0)


def gather_and_reduce(
    offsets, panels, eig, tf, H, YT, E,
    pbuf, tfbuf, T, gt, ws, cbuf, xs, zbuf, cg, crow, Cq,
    local_sem, a_send, a_recv, b_send, b_recv,
    w_send, w_recv, z_send, z_recv, g_send, g_recv, c_send, c_recv, y_send, y_recv, s_send, s_recv,
):
    col = lax.axis_index("col")
    row = lax.axis_index("row")
    x, y = col % NX, col // NX
    z, core = row // 2, row % 2

    def at_x(d):
        return {"col": y * NX + (x + d) % NX}

    def at_y(d):
        return {"col": ((y + d) % NX) * NX + x}

    def at_z(d):
        return {"row": ((z + d) % NZ) * 2 + core}

    sibling = {"row": z * 2 + (1 - core)}

    load_panels = pltpu.make_async_copy(panels, pbuf, local_sem.at[0])
    load_tf = pltpu.make_async_copy(tf, tfbuf, local_sem.at[1])
    load_eig = pltpu.make_async_copy(eig, E, local_sem.at[2])
    load_panels.start()
    load_tf.start()
    load_eig.start()

    Cq[...] = jnp.zeros((Q, Q), F32)
    barrier = pltpu.get_barrier_semaphore()
    for d in range(1, 16):
        pl.semaphore_signal(barrier, inc=1, device_id={"col": (col + d) % 16}, device_id_type=MESH)
        pl.semaphore_signal(barrier, inc=1, device_id={"row": (row + d) % 16}, device_id_type=MESH)

    slot = pl.multiple_of((x * NX + y) * OWN, OWN)
    load_panels.wait()
    step = 512
    for c0 in range(0, RD, step):
        position = row * RD + c0 + lax.broadcasted_iota(jnp.int32, (8, step), 1)
        parts = []
        for p in range(2):
            pivot = offsets[p] + col * 8 + lax.broadcasted_iota(jnp.int32, (8, step), 0)
            v = pbuf[p, :, c0 : c0 + step].astype(F32)
            parts.append(jnp.where(position > pivot, v, jnp.where(position == pivot, 1.0, 0.0)))
        H[pl.ds(slot, OWN), c0 : c0 + step] = jnp.concatenate(parts, axis=0).astype(BF16)

    pl.semaphore_wait(barrier, 30)

    def part(dx, dy, lo, n):
        s = ((x + dx) % NX) * NX + (y + dy) % NX
        return H.at[pl.ds(pl.multiple_of(s * OWN, OWN), OWN), lo : lo + n]

    sent = []

    def send(ref, sems, i, dev):
        send_sem, recv_sem = sems
        cp = pltpu.make_async_remote_copy(ref, ref, send_sem.at[i], recv_sem.at[i], device_id=dev, device_id_type=MESH)
        cp.start()
        sent.append(cp)

    def recv(ref, sems, i):
        send_sem, recv_sem = sems
        pltpu.make_async_remote_copy(ref, ref, send_sem.at[i], recv_sem.at[i], device_id=sibling, device_id_type=MESH).wait_recv()

    class Half:
        def __init__(self, lo, sems, first, second, turn):
            self.lo, self.sems, self.first, self.second, self.turn = lo, sems, first, second, turn

        def ref(self, d1, d2, piece=None):
            lo, n = (self.lo, HALF) if piece is None else (self.lo + piece * QUART, QUART)
            return part(d1, d2, lo, n) if not self.turn else part(d2, d1, lo, n)

        def send_own(self):
            send(self.ref(0, 0), self.sems, 0, self.first(1))
            send(self.ref(0, 0), self.sems, 1, self.first(-1))

        def recv_own(self):
            recv(self.ref(-1, 0), self.sems, 0)
            recv(self.ref(1, 0), self.sems, 1)

        def send_far(self):
            send(self.ref(-1, 0, 0), self.sems, 2, self.first(1))
            send(self.ref(1, 0, 1), self.sems, 3, self.first(-1))

        def recv_far(self):
            recv(self.ref(2, 0, 0), self.sems, 2)
            recv(self.ref(2, 0, 1), self.sems, 3)

        def send_line(self, d):
            send(self.ref(d, 0), self.sems, 4 + 2 * d, self.second(1))
            send(self.ref(d, 0), self.sems, 5 + 2 * d, self.second(-1))

        def recv_line(self, d):
            recv(self.ref(d, -1), self.sems, 4 + 2 * d)
            recv(self.ref(d, 1), self.sems, 5 + 2 * d)

        def send_far_line(self, d):
            send(self.ref(d, -1, 0), self.sems, 12 + 2 * d, self.second(1))
            send(self.ref(d, 1, 1), self.sems, 13 + 2 * d, self.second(-1))

        def recv_far_line(self, d):
            recv(self.ref(d, 2, 0), self.sems, 12 + 2 * d)
            recv(self.ref(d, 2, 1), self.sems, 13 + 2 * d)

    a = Half(0, (a_send, a_recv), at_x, at_y, False)
    b = Half(HALF, (b_send, b_recv), at_y, at_x, True)

    def products(k):
        dx = ORDER[k]
        r0 = pl.multiple_of(((x + dx) % NX) * CHUNK, CHUNK)
        ws[k] = jnp.zeros((CHUNK, KD), F32)
        gt[pl.ds(r0, CHUNK), :] = jnp.zeros((CHUNK, OWN), F32)

        def body(t, _):
            k0 = pl.multiple_of(t * KT, KT)
            h = H[pl.ds(r0, CHUNK), pl.ds(k0, KT)]
            ws[k] += jnp.dot(h, E[pl.ds(k0, KT), :], preferred_element_type=F32)
            own = H[pl.ds(slot, OWN), pl.ds(k0, KT)]
            gt[pl.ds(r0, CHUNK), :] += lax.dot_general(h, own, (((1,), (1,)), ((), ())), preferred_element_type=F32)
            return 0

        lax.fori_loop(0, RD // KT, body, 0)
        theirs = pl.ds(pl.multiple_of((1 - core) * (KD // 2), KD // 2), KD // 2)
        cp = pltpu.make_async_remote_copy(
            ws.at[k, :, theirs], cbuf.at[k], w_send.at[k], w_recv.at[k], device_id=sibling, device_id_type=MESH
        )
        cp.start()
        sent.append(cp)

    def scatter(k):
        pltpu.make_async_remote_copy(
            cbuf.at[k], cbuf.at[k], w_send.at[k], w_recv.at[k], device_id=sibling, device_id_type=MESH
        ).wait_recv()
        mine = pl.ds(pl.multiple_of(core * (KD // 2), KD // 2), KD // 2)
        s = ws[k, :, mine] + cbuf[k]
        xs[k] = jnp.concatenate([s[:, :128], s[:, 128:]], axis=0).T
        for d in range(1, NZ):
            r = pl.multiple_of(((z + d) % NZ) * 16, 16)
            cp = pltpu.make_async_remote_copy(
                xs.at[k, pl.ds(r, 16)], zbuf.at[k, d], z_send.at[k, d], z_recv.at[k, d],
                device_id=at_z(d), device_id_type=MESH,
            )
            cp.start()
            sent.append(cp)

    def collect(k):
        total = xs[k, pl.ds(pl.multiple_of(z * 16, 16), 16)]
        for d in range(1, NZ):
            ref = zbuf.at[k, d]
            pltpu.make_async_remote_copy(
                ref, ref, z_send.at[k, d], z_recv.at[k, d], device_id=sibling, device_id_type=MESH
            ).wait_recv()
            total = total + zbuf[k, d]
        return total

    a.send_own()
    b.send_own()
    a.send_line(0)
    b.send_line(0)
    load_tf.wait()
    for p in range(2):
        tri = lax.broadcasted_iota(jnp.int32, (NB, NB), 0) <= lax.broadcasted_iota(jnp.int32, (NB, NB), 1)
        u = jnp.where(tri, tfbuf[p], 0.0)
        T[p] = expand(expand(u, p).T, p)
    a.recv_own()
    a.send_far()
    a.send_line(1)
    a.send_line(3)
    b.recv_own()
    b.send_far()
    b.send_line(1)
    b.send_line(3)
    a.recv_line(0)
    a.send_far_line(0)
    b.recv_far()
    b.send_line(2)
    b.recv_line(0)
    b.send_far_line(0)
    load_eig.wait()
    a.recv_far_line(0)
    products(0)
    a.recv_line(1)
    a.send_far_line(1)
    a.recv_line(3)
    a.send_far_line(3)
    a.recv_far()
    a.send_line(2)
    b.recv_line(1)
    b.send_far_line(1)
    b.recv_line(3)
    b.send_far_line(3)
    scatter(0)
    b.recv_line(2)
    b.send_far_line(2)
    a.recv_far_line(1)
    products(1)
    a.recv_line(2)
    a.send_far_line(2)
    a.recv_far_line(3)
    products(2)
    scatter(1)
    scatter(2)
    a.recv_far_line(2)
    for d in range(NX):
        b.recv_far_line(d)
    products(3)

    cg[...] = gt[...].T[:8, :]
    for d in range(1, 16):
        cp = pltpu.make_async_remote_copy(
            cg, crow.at[d], g_send.at[d], g_recv.at[d], device_id={"row": (row + d) % 16}, device_id_type=MESH
        )
        cp.start()
        sent.append(cp)
    scatter(3)
    total = cg[...]
    for d in range(1, 16):
        ref = crow.at[d]
        pltpu.make_async_remote_copy(
            ref, ref, g_send.at[d], g_recv.at[d], device_id=sibling, device_id_type=MESH
        ).wait_recv()
        total = total + crow[d]
    Cq[pl.ds(slot, 8), :] = total

    def cross_rows(d):
        o = (col + 16 - d) % 16
        return Cq.at[pl.ds(pl.multiple_of(((o % NX) * NX + o // NX) * OWN, OWN), 8), :]

    for d in range(1, 16):
        cp = pltpu.make_async_remote_copy(
            cross_rows(0), cross_rows(0), c_send.at[d], c_recv.at[d],
            device_id={"col": (col + d) % 16}, device_id_type=MESH,
        )
        cp.start()
        sent.append(cp)

    by_chunk = {ORDER[k]: collect(k) for k in range(NX)}
    wt = jnp.concatenate(
        [jnp.concatenate([by_chunk[d][:, h * 64 : h * 64 + 64] for d in range(NX)], axis=1) for h in range(2)], axis=0
    )
    wt = pltpu.roll(wt, x * CHUNK, 1)
    y1 = jnp.dot(wt, T[1], precision=HIGH, preferred_element_type=F32).astype(BF16).astype(F32)
    for d in range(1, 16):
        ref = cross_rows(d)
        pltpu.make_async_remote_copy(
            ref, ref, c_send.at[d], c_recv.at[d], device_id=sibling, device_id_type=MESH
        ).wait_recv()
    w0 = wt - lax.dot_general(y1, Cq[...], (((1,), (1,)), ((), ())), precision=HIGH, preferred_element_type=F32)
    y0 = jnp.dot(w0, T[0], precision=HIGH, preferred_element_type=F32)
    yt = (y1 + y0).astype(BF16)

    def shift_rows(dz, h):
        return YT.at[pl.ds(pl.multiple_of(core * 256 + h * 128 + ((z + dz) % NZ) * 16, 16), 16), :]

    for h in range(2):
        YT[pl.ds(pl.multiple_of(core * 256 + h * 128 + z * 16, 16), 16), :] = yt[h * 16 : h * 16 + 16]
        for d in range(1, NZ):
            ref = shift_rows(0, h)
            cp = pltpu.make_async_remote_copy(
                ref, ref, y_send.at[h, d], y_recv.at[h, d], device_id=at_z(d), device_id_type=MESH
            )
            cp.start()
            sent.append(cp)
    for h in range(2):
        for d in range(1, NZ):
            ref = shift_rows(-d, h)
            pltpu.make_async_remote_copy(
                ref, ref, y_send.at[h, d], y_recv.at[h, d], device_id=sibling, device_id_type=MESH
            ).wait_recv()
    ours = YT.at[pl.ds(pl.multiple_of(core * 256, 256), 256), :]
    theirs = YT.at[pl.ds(pl.multiple_of((1 - core) * 256, 256), 256), :]
    cp = pltpu.make_async_remote_copy(ours, ours, s_send, s_recv, device_id=sibling, device_id_type=MESH)
    cp.start()
    sent.append(cp)
    pltpu.make_async_remote_copy(theirs, theirs, s_send, s_recv, device_id=sibling, device_id_type=MESH).wait_recv()
    for cp in sent:
        cp.wait_send()


ROWS = 1024


def apply_shift(H, YT, E, out, shift):
    i = pl.program_id(0)

    @pl.when(i == 0)
    def _():
        shift[...] = YT[...].T

    rows = pl.ds(pl.multiple_of(i * ROWS, ROWS), ROWS)
    term = lax.dot_general(H[:, rows], shift[...], (((0,), (0,)), ((), ())), preferred_element_type=F32)
    out[...] = (E[rows, :].astype(F32) - term).astype(BF16)


def local(eigvecs, panels, tfactors, offsets):
    anywhere = pl.BlockSpec(memory_space=pl.ANY)
    dma = pltpu.SemaphoreType.DMA
    H, YT, E = pl.pallas_call(
        gather_and_reduce,
        out_shape=[
            pltpu.VMEM((Q, RD), BF16),
            pltpu.VMEM((KD, Q), BF16),
            pltpu.VMEM((RD, KD), BF16),
        ],
        in_specs=[pl.BlockSpec(memory_space=pltpu.SMEM), anywhere, anywhere, anywhere],
        out_specs=[pl.BlockSpec(memory_space=pltpu.VMEM)] * 3,
        scratch_shapes=[
            pltpu.VMEM((2, 8, RD), BF16),
            pltpu.VMEM((2, NB, NB), F32),
            pltpu.VMEM((2, Q, Q), F32),
            pltpu.VMEM((Q, OWN), F32),
            pltpu.VMEM((NX, CHUNK, KD), F32),
            pltpu.VMEM((NX, CHUNK, KD // 2), F32),
            pltpu.VMEM((NX, 128, 128), F32),
            pltpu.VMEM((NX, NZ, 16, 128), F32),
            pltpu.VMEM((8, Q), F32),
            pltpu.VMEM((16, 8, Q), F32),
            pltpu.VMEM((Q, Q), F32),
            dma((3,)),
            dma((20,)), dma((20,)), dma((20,)), dma((20,)),
            dma((NX,)), dma((NX,)),
            dma((NX, NZ)), dma((NX, NZ)),
            dma((16,)), dma((16,)), dma((16,)), dma((16,)),
            dma((2, NZ)), dma((2, NZ)),
            dma, dma,
        ],
        compiler_params=pltpu.CompilerParams(
            collective_id=0, has_side_effects=True, vmem_limit_bytes=40 * 1024 * 1024
        ),
        name="gather_and_reduce",
    )(offsets, panels, eigvecs, tfactors)
    whole = pl.BlockSpec(memory_space=pltpu.VMEM)
    return pl.pallas_call(
        apply_shift,
        grid=(RD // ROWS,),
        out_shape=jax.ShapeDtypeStruct((RD, KD), BF16),
        in_specs=[whole, whole, whole],
        out_specs=pl.BlockSpec((ROWS, KD), lambda i: (i, 0)),
        scratch_shapes=[pltpu.VMEM((Q, KD), BF16)],
        compiler_params=pltpu.CompilerParams(vmem_limit_bytes=40 * 1024 * 1024),
        name="apply_shift",
    )(H, YT, E)


def solution(mesh):
    return jax.shard_map(
        local,
        mesh=mesh,
        in_specs=(P("row", "col"), P(None, "col", "row"), P(), P()),
        out_specs=P("row", "col"),
        check_vma=False,
    )
```

time: 306 us -> 67.9 us (0.22)
  waiting for transfers between devices: 265 us -> 0 us
  Pallas kernels: 0 us -> 65.3 us
  matrix products: 19.3 us -> 0 us
  between operations: 13.2 us -> 0.01 us
  other arithmetic: 5.52 us -> 0 us
    psum x2 -> x0, waiting for transfers between devices: 209 us -> none  [the longest x1 109 us: local(): coeff_zero = lax.psum(term_zero, 'row')]
    pallas_call x0 -> x2, Pallas kernels: none -> 65.3 us  [the longest x1 60.2 us: local(): pl.pallas_call(gather_and_reduce, out_shape=[pltpu.VMEM((Q, RD), BF16), p...]
    all_gather x1 -> x0, waiting for transfers between devices: 55.3 us -> none  [local(): whole = lax.all_gather(panels, 'col', axis=1, tiled=True)]
    dot_general x7 -> x0, matrix products: 19.3 us -> none  [the longest x1 5.63 us: local(): lax.dot_general(stacked, shifts, dims, preferred_element_type=jnp.float32)]
    select_n x2 -> x0, other arithmetic: 4.14 us -> none  [the longest x1 3.22 us: reflector(): return jnp.where(position > pivot, whole[p], unit)]
  transfers between devices with their start and end apart: 3 -> 0, of which waited for: 3 -> 0; matrix products, arithmetic and copies ran while one was open for 4% -> 0% of each run, Pallas kernels for 0% -> 0%
where the time goes in v1:
time: 67.9 us; the launch traced here: 67.8 us
  Pallas kernels  65.3 us (96%)
  local copies, waits for them, and re-layouts  2.48 us (4%)
    pallas_call x1, Pallas kernels, local(): pl.pallas_call(gather_and_reduce, out_shape=[pltpu.VMEM((Q, RD), BF16), p...  60.2 us
    pallas_call x1, Pallas kernels, local(): pl.pallas_call(apply_shift, grid=(RD // ROWS,), out_shape=jax.ShapeDtypeS...  5.01 us
    unnamed x6, local copies, waits for them, and re-layouts  2.48 us

profile of v1, /device:TPU:1, one launch (start us, length us, event | category | flops | bytes accessed | tf_op | source)
XLA Modules:
  0.0 67.8 jit_solution(15410094237002016233)
XLA Ops:
  0.0 0.0 copy-start
  0.0 0.9 %copy-done = bf16[2,8,6144]{2,1,0:T(8,128)(2,1)S(1)} copy-done((bf16[2,8,6144]{2,1,0:T(8,128)(2,1)S(1)}, bf16[2,8,6144]{2,1,0:T(8,128)(2,1)}, u32[]{:S(2)}) %copy-start) | copy-done | bytes 196632
  0.9 0.0 copy-start.1
  0.9 0.9 %copy-done.1 = f32[2,128,128]{2,1,0:T(8,128)S(1)} copy-done((f32[2,128,128]{2,1,0:T(8,128)S(1)}, f32[2,128,128]{2,1,0:T(8,128)}, u32[]{:S(2)}) %copy-start.1) | copy-done | bytes 131096
  1.8 0.0 copy-start.2
  1.8 0.7 copy-done.2
  2.5 60.2 %gather_and_reduce.1 = (bf16[256,6144]{1,0:T(8,128)(2,1)S(1)}, bf16[512,256]{1,0:T(8,128)(2,1)S(1)}, bf16[6144,512]{1,0:T(8,128)(2,1)S(1)}) custom-call(s32[2]{0:T(128)S(1)} %copy-done.2, bf16[2,8,6144]{2,1,0:T(8,128)(2,1)S(1)} %copy-done, bf16[6144,512]{1,0:T(8,128)(2,1)} %eig.1, f32[2,128,128]{2,1,0:T(8,128)S(1)} %copy-done.1), custom_call_target="tpu_custom_call" | custom-call | tf_op jit(solution)/shard_map/gather_and_reduce/pallas_call | solution.py:337
  62.7 5.0 %apply_shift.1 = bf16[6144,512]{1,0:T(8,128)(2,1)} custom-call(bf16[256,6144]{1,0:T(8,128)(2,1)S(1)} %get-tuple-element.8.H, bf16[512,256]{1,0:T(8,128)(2,1)S(1)} %get-tuple-element.9.YT, bf16[6144,512]{1,0:T(8,128)(2,1)S(1)} %get-tuple-element.10.E), custom_call_target="tpu_custom_call" | custom-call | tf_op jit(solution)/shard_map/apply_shift/pallas_call | solution.py:372
Async XLA Ops:
  0.0 0.9 %copy-start = (bf16[2,8,6144]{2,1,0:T(8,128)(2,1)S(1)}, bf16[2,8,6144]{2,1,0:T(8,128)(2,1)}, u32[]{:S(2)}) copy-start(bf16[2,8,6144]{2,1,0:T(8,128)(2,1)} %panels.1) | copy-start | bytes 589828
  0.9 0.9 %copy-start.1 = (f32[2,128,128]{2,1,0:T(8,128)S(1)}, f32[2,128,128]{2,1,0:T(8,128)}, u32[]{:S(2)}) copy-start(f32[2,128,128]{2,1,0:T(8,128)} %tf.1) | copy-start | bytes 393220
  1.8 0.7 copy-start.2

commit v2 on v0

v2 whole, which is shorter than its diff:
```python
import jax
import jax.numpy as jnp
from jax import lax
from jax.experimental import pallas as pl
from jax.experimental.pallas import tpu as pltpu
from jax.sharding import PartitionSpec as P

MESH = pl.DeviceIdType.MESH
F32 = jnp.float32
BF16 = jnp.bfloat16
HIGH = lax.Precision.HIGHEST

NB = 128
RD = 6144
KD = 512
KH = KD // 2
NX = 4
NZ = 8
OWN = 8
SLOTS = NX * NX
HALF = RD // 2
QUART = RD // 4
CHUNK = NX * OWN
KT = 1536
ORDER = (0, 1, 3, 2)


def dot(a, b, dims=((1,), (0,)), precision=None):
    return lax.dot_general(a, b, (dims, ((), ())), precision=precision, preferred_element_type=F32)


def by_place(a):
    return jnp.concatenate([a[(sy * NX + sx) * OWN :][:OWN, :] for sx in range(NX) for sy in range(NX)], axis=0)


def gather_and_reduce(
    offsets, panels, eig, tf, HT, Y, E,
    H, obuf, pbuf, tfbuf, T, ct, w1, c1, x1, z1, w0, c0, x0, z0, crow, C, ybuf,
    local_sem, a_send, a_recv, b_send, b_recv,
    w_send, w_recv, z_send, z_recv, g_send, g_recv, c_send, c_recv, y_send, y_recv, f_send, f_recv,
):
    col = lax.axis_index("col")
    row = lax.axis_index("row")
    x, y = col % NX, col // NX
    z, core = row // 2, row % 2

    def at_x(d):
        return {"col": y * NX + (x + d) % NX}

    def at_y(d):
        return {"col": ((y + d) % NX) * NX + x}

    def at_z(d):
        return {"row": ((z + d) % NZ) * 2 + core}

    sibling = {"row": z * 2 + (1 - core)}

    load_panels = pltpu.make_async_copy(panels, pbuf, local_sem.at[0])
    load_offsets = pltpu.make_async_copy(offsets, obuf, local_sem.at[3])
    load_tf = pltpu.make_async_copy(tf, tfbuf, local_sem.at[1])
    load_eig = pltpu.make_async_copy(eig, E, local_sem.at[2])
    load_panels.start()
    load_offsets.start()
    load_tf.start()
    load_eig.start()

    barrier = pltpu.get_barrier_semaphore()
    for d in range(1, 16):
        pl.semaphore_signal(barrier, inc=1, device_id={"col": (col + d) % 16}, device_id_type=MESH)
        pl.semaphore_signal(barrier, inc=1, device_id={"row": (row + d) % 16}, device_id_type=MESH)

    slot = x * NX + y
    load_panels.wait()
    load_offsets.wait()
    step = 512
    for p in range(2):
        pivot = obuf[p] + col * OWN + lax.broadcasted_iota(jnp.int32, (OWN, step), 0)
        for s in range(0, RD, step):
            position = row * RD + s + lax.broadcasted_iota(jnp.int32, (OWN, step), 1)
            v = pbuf[p, :, s : s + step].astype(F32)
            v = jnp.where(position > pivot, v, jnp.where(position == pivot, 1.0, 0.0))
            H[p, slot, :, s : s + step] = v.astype(BF16)

    pl.semaphore_wait(barrier, 30)

    def part(p, dx, dy, lo, n):
        return H.at[p, ((x + dx) % NX) * NX + (y + dy) % NX, :, lo : lo + n]

    sent = []

    def send(src, dst, send_sem, recv_sem, dev):
        cp = pltpu.make_async_remote_copy(src, dst, send_sem, recv_sem, device_id=dev, device_id_type=MESH)
        cp.start()
        sent.append(cp)

    def recv(ref, send_sem, recv_sem):
        pltpu.make_async_remote_copy(
            ref, ref, send_sem, recv_sem, device_id=sibling, device_id_type=MESH
        ).wait_recv()

    class Half:
        def __init__(self, p, lo, sems, first, second, turn):
            self.p, self.lo, self.sems = p, lo, sems
            self.first, self.second, self.turn = first, second, turn

        def ref(self, d1, d2, piece=None):
            lo, n = (self.lo, HALF) if piece is None else (self.lo + piece * QUART, QUART)
            return part(self.p, d2, d1, lo, n) if self.turn else part(self.p, d1, d2, lo, n)

        def put(self, ref, i, dev):
            send(ref, ref, self.sems[0].at[self.p, i], self.sems[1].at[self.p, i], dev)

        def get(self, ref, i):
            recv(ref, self.sems[0].at[self.p, i], self.sems[1].at[self.p, i])

        def send_own(self):
            self.put(self.ref(0, 0), 0, self.first(1))
            self.put(self.ref(0, 0), 1, self.first(-1))

        def recv_own(self):
            self.get(self.ref(-1, 0), 0)
            self.get(self.ref(1, 0), 1)

        def send_far(self):
            self.put(self.ref(-1, 0, 0), 2, self.first(1))
            self.put(self.ref(1, 0, 1), 3, self.first(-1))

        def recv_far(self):
            self.get(self.ref(2, 0, 0), 2)
            self.get(self.ref(2, 0, 1), 3)

        def send_line(self, d):
            self.put(self.ref(d, 0), 4 + 2 * d, self.second(1))
            self.put(self.ref(d, 0), 5 + 2 * d, self.second(-1))

        def recv_line(self, d):
            self.get(self.ref(d, -1), 4 + 2 * d)
            self.get(self.ref(d, 1), 5 + 2 * d)

        def send_far_line(self, d):
            self.put(self.ref(d, -1, 0), 12 + 2 * d, self.second(1))
            self.put(self.ref(d, 1, 1), 13 + 2 * d, self.second(-1))

        def recv_far_line(self, d):
            self.get(self.ref(d, 2, 0), 12 + 2 * d)
            self.get(self.ref(d, 2, 1), 13 + 2 * d)

        def own_on(self):
            self.recv_own()
            self.send_far()
            self.send_line(1)
            self.send_line(3)

        def line_on(self, *ds):
            for d in ds:
                self.recv_line(d)
                self.send_far_line(d)

        def far_on(self):
            self.recv_far()
            self.send_line(2)

    halves = {
        p: (
            Half(p, 0, (a_send, a_recv), at_x, at_y, False),
            Half(p, HALF, (b_send, b_recv), at_y, at_x, True),
        )
        for p in range(2)
    }
    a0, b0 = halves[0]
    a1, b1 = halves[1]

    theirs = pl.ds(pl.multiple_of((1 - core) * KH, KH), KH)
    mine = pl.ds(pl.multiple_of(core * KH, KH), KH)

    def products_one():
        for t in range(RD // KT):
            k = slice(t * KT, (t + 1) * KT)
            h = H[1, :, :, k].reshape(NB, KT)
            s = dot(h, E[k, :])
            c = dot(h, H[0, slot, :, k], ((1,), (1,)))
            if t:
                s, c = s + w1[...], c + ct[...]
            w1[...] = s
            ct[...] = c
        crow[0] = ct[...].T
        for d in range(1, 16):
            send(crow.at[0], crow.at[d], g_send.at[d], g_recv.at[d], {"row": (row + d) % 16})
        send(w1.at[:, theirs], c1, w_send.at[NX], w_recv.at[NX], sibling)

    def scatter_one():
        recv(c1, w_send.at[NX], w_recv.at[NX])
        x1[...] = (w1[:, mine] + c1[...]).T.reshape(4, 64, NB)
        for d in (4, 3, 5, 2, 6, 1, 7):
            r = pl.multiple_of(((z + d) % NZ) * 8, 8)
            send(x1.at[:, pl.ds(r, 8), :], z1.at[d], z_send.at[NX, d], z_recv.at[NX, d], at_z(d))

    def collect_one():
        total = x1[:, pl.ds(pl.multiple_of(z * 8, 8), 8), :]
        for d in range(1, NZ):
            recv(z1.at[d], z_send.at[NX, d], z_recv.at[NX, d])
            total = total + z1[d]
        return total.reshape(32, NB)

    def products(k, lo, hi):
        sx = (x + ORDER[k]) % NX
        for t in range(lo // KT, hi // KT):
            ks = slice(t * KT, (t + 1) * KT)
            s = dot(H[0, pl.ds(sx * NX, NX), :, ks].reshape(CHUNK, KT), E[ks, :])
            w0[k] = s + w0[k] if t else s

    def swap(k):
        send(w0.at[k, :, theirs], c0.at[k], w_send.at[k], w_recv.at[k], sibling)

    def scatter(k):
        recv(c0.at[k], w_send.at[k], w_recv.at[k])
        s = w0[k, :, mine] + c0[k]
        x0[k] = jnp.concatenate([s[:, g * 64 : g * 64 + 64] for g in range(4)], axis=0).T
        for d in (4, 3, 5, 2, 6, 1, 7):
            r = pl.multiple_of(((z + d) % NZ) * 8, 8)
            send(x0.at[k, pl.ds(r, 8), :], z0.at[k, d], z_send.at[k, d], z_recv.at[k, d], at_z(d))

    def collect(k):
        total = x0[k, pl.ds(pl.multiple_of(z * 8, 8), 8), :]
        for d in range(1, NZ):
            recv(z0.at[k, d], z_send.at[k, d], z_recv.at[k, d])
            total = total + z0[k, d]
        return jnp.concatenate([total[:, g * CHUNK : (g + 1) * CHUNK] for g in range(4)], axis=0)

    def cross_sum():
        total = crow[0]
        for d in range(1, 16):
            recv(crow.at[d], g_send.at[d], g_recv.at[d])
            total = total + crow[d]
        C[slot] = total
        for d in range(1, 16):
            send(C.at[slot], C.at[slot], c_send.at[d], c_recv.at[d], {"col": (col + d) % 16})

    def cross_recv():
        for d in range(1, 16):
            o = (col + 16 - d) % 16
            recv(C.at[(o % NX) * NX + o // NX], c_send.at[d], c_recv.at[d])
        return C[...].reshape(NB, NB)

    def spread(p, value):
        ref = ybuf.at[p, core * NZ + z]
        ybuf[p, core * NZ + z] = value
        for d in (4, 3, 5, 2, 6, 1, 7):
            send(ref, ref, y_send.at[p, d], y_recv.at[p, d], at_z(d))
        send(ref, ref, f_send.at[p, 0], f_recv.at[p, 0], sibling)

    def pass_on(p):
        for d in (1, 7, 2, 6, 3, 5, 4):
            ref = ybuf.at[p, core * NZ + (z + NZ - d) % NZ]
            recv(ref, y_send.at[p, d], y_recv.at[p, d])
            send(ref, ref, f_send.at[p, d], f_recv.at[p, d], sibling)

    def place(p, c):
        v = [ybuf[p, c * NZ + i].astype(F32) for i in range(NZ)]
        v = jnp.concatenate([v[i][g * 8 : g * 8 + 8, :] for g in range(4) for i in range(NZ)], axis=0)
        Y[p * NB : (p + 1) * NB, pl.ds(pl.multiple_of(c * KH, KH), KH)] = v.T.astype(BF16)

    def finish(p):
        place(p, core)
        for d in range(NZ):
            recv(ybuf.at[p, (1 - core) * NZ + (z + NZ - d) % NZ], f_send.at[p, d], f_recv.at[p, d])
        place(p, 1 - core)

    def turn(p):
        for r in range(0, RD, 512):
            HT[r : r + 512, p * NB : (p + 1) * NB] = H[p, :, :, r : r + 512].reshape(NB, 512).T

    a1.send_own()
    b1.send_own()
    a1.send_line(0)
    b1.send_line(0)
    load_tf.wait()
    for p in range(2):
        tri = lax.broadcasted_iota(jnp.int32, (NB, NB), 0) <= lax.broadcasted_iota(jnp.int32, (NB, NB), 1)
        T[p] = by_place(by_place(jnp.where(tri, tfbuf[p], 0.0)).T)
    a0.send_own()
    b0.send_own()
    a0.send_line(0)
    b0.send_line(0)
    a1.own_on()
    b1.own_on()
    a1.line_on(0)
    b1.line_on(0)
    a1.far_on()
    b1.far_on()
    a0.own_on()
    b0.own_on()
    a1.line_on(1, 3)
    b1.line_on(1, 3)
    a0.line_on(0)
    b0.line_on(0)
    a1.line_on(2)
    b1.line_on(2)
    a0.far_on()
    b0.far_on()
    a0.line_on(1, 3)
    b0.line_on(1, 3)
    load_eig.wait()
    for d in range(NX):
        a1.recv_far_line(d)
        b1.recv_far_line(d)
    products_one()
    a0.line_on(2)
    b0.line_on(2)
    scatter_one()
    a0.recv_far_line(0)
    products(0, 0, RD)
    swap(0)
    a0.recv_far_line(1)
    products(1, 0, RD)
    swap(1)
    cross_sum()
    a0.recv_far_line(3)
    products(2, 0, RD)
    swap(2)
    scatter(0)
    scatter(1)
    a0.recv_far_line(2)
    products(3, 0, HALF)
    for d in range(NX):
        b0.recv_far_line(d)
    products(3, HALF, RD)
    swap(3)
    scatter(2)
    y1 = dot(collect_one(), T[1], precision=HIGH).astype(BF16)
    spread(1, y1)
    scatter(3)
    turn(1)
    turn(0)
    cross = cross_recv()
    shift = dot(y1.astype(F32), cross, ((1,), (1,)), precision=HIGH)
    parts = {ORDER[k]: collect(k) for k in range(NX)}
    total = pltpu.roll(jnp.concatenate([parts[d] for d in range(NX)], axis=1), x * CHUNK, 1)
    spread(0, dot(total - shift, T[0], precision=HIGH).astype(BF16))
    pass_on(1)
    finish(1)
    pass_on(0)
    finish(0)
    for cp in sent:
        cp.wait_send()


ROWS = 1024


def apply_shift(HT, Y, E, out):
    rows = pl.ds(pl.multiple_of(pl.program_id(0) * ROWS, ROWS), ROWS)
    out[...] = (E[rows, :].astype(F32) - dot(HT[rows, :], Y[...])).astype(BF16)


def local(eigvecs, panels, tfactors, offsets):
    hbm = pl.BlockSpec(memory_space=pltpu.HBM)
    dma = pltpu.SemaphoreType.DMA
    HT, Y, E = pl.pallas_call(
        gather_and_reduce,
        out_shape=[
            pltpu.VMEM((RD, 2 * NB), BF16),
            pltpu.VMEM((2 * NB, KD), BF16),
            pltpu.VMEM((RD, KD), BF16),
        ],
        in_specs=[hbm] * 4,
        out_specs=[pl.BlockSpec(memory_space=pltpu.VMEM)] * 3,
        scratch_shapes=[
            pltpu.VMEM((2, SLOTS, OWN, RD), BF16),
            pltpu.SMEM((2,), jnp.int32),
            pltpu.VMEM((2, OWN, RD), BF16),
            pltpu.VMEM((2, NB, NB), F32),
            pltpu.VMEM((2, NB, NB), F32),
            pltpu.VMEM((NB, OWN), F32),
            pltpu.VMEM((NB, KD), F32),
            pltpu.VMEM((NB, KH), F32),
            pltpu.VMEM((4, 64, NB), F32),
            pltpu.VMEM((NZ, 4, 8, NB), F32),
            pltpu.VMEM((NX, CHUNK, KD), F32),
            pltpu.VMEM((NX, CHUNK, KH), F32),
            pltpu.VMEM((NX, 64, 128), F32),
            pltpu.VMEM((NX, NZ, 8, 128), F32),
            pltpu.VMEM((16, OWN, NB), F32),
            pltpu.VMEM((SLOTS, OWN, NB), F32),
            pltpu.VMEM((2, 16, 32, NB), BF16),
            dma((4,)),
            dma((2, 20)), dma((2, 20)), dma((2, 20)), dma((2, 20)),
            dma((NX + 1,)), dma((NX + 1,)),
            dma((NX + 1, NZ)), dma((NX + 1, NZ)),
            dma((16,)), dma((16,)), dma((16,)), dma((16,)),
            dma((2, NZ)), dma((2, NZ)),
            dma((2, NZ)), dma((2, NZ)),
        ],
        compiler_params=pltpu.CompilerParams(
            collective_id=0, has_side_effects=True, vmem_limit_bytes=40 * 1024 * 1024
        ),
        name="gather_and_reduce",
    )(*(pltpu.with_memory_space_constraint(v, pltpu.HBM) for v in (offsets, panels, eigvecs, tfactors)))
    whole = pl.BlockSpec(memory_space=pltpu.VMEM)
    return pl.pallas_call(
        apply_shift,
        grid=(RD // ROWS,),
        out_shape=jax.ShapeDtypeStruct((RD, KD), BF16),
        in_specs=[whole, whole, whole],
        out_specs=pl.BlockSpec((ROWS, KD), lambda i: (i, 0)),
        compiler_params=pltpu.CompilerParams(vmem_limit_bytes=40 * 1024 * 1024),
        name="apply_shift",
    )(HT, Y, E)


def solution(mesh):
    return jax.shard_map(
        local,
        mesh=mesh,
        in_specs=(P("row", "col"), P(None, "col", "row"), P(), P()),
        out_specs=P("row", "col"),
        check_vma=False,
    )
```

time: 306 us -> 58.8 us (0.19)
  waiting for transfers between devices: 265 us -> 0 us
  Pallas kernels: 0 us -> 58.7 us
  matrix products: 19.3 us -> 0 us
  between operations: 13.2 us -> 0.01 us
  other arithmetic: 5.52 us -> 0 us
    psum x2 -> x0, waiting for transfers between devices: 209 us -> none  [the longest x1 109 us: local(): coeff_zero = lax.psum(term_zero, 'row')]
    pallas_call x0 -> x2, Pallas kernels: none -> 58.7 us  [the longest x1 54 us: local(): pl.pallas_call(gather_and_reduce, out_shape=[pltpu.VMEM((RD, 2 * NB), BF1...]
    all_gather x1 -> x0, waiting for transfers between devices: 55.3 us -> none  [local(): whole = lax.all_gather(panels, 'col', axis=1, tiled=True)]
    dot_general x7 -> x0, matrix products: 19.3 us -> none  [the longest x1 5.63 us: local(): lax.dot_general(stacked, shifts, dims, preferred_element_type=jnp.float32)]
    select_n x2 -> x0, other arithmetic: 4.14 us -> none  [the longest x1 3.22 us: reflector(): return jnp.where(position > pivot, whole[p], unit)]
  transfers between devices with their start and end apart: 3 -> 0, of which waited for: 3 -> 0; matrix products, arithmetic and copies ran while one was open for 4% -> 0% of each run, Pallas kernels for 0% -> 0%
where the time goes in v2:
time: 58.8 us; the launch traced here: 58.7 us
  Pallas kernels  58.7 us (100%)
    pallas_call x1, Pallas kernels, local(): pl.pallas_call(gather_and_reduce, out_shape=[pltpu.VMEM((RD, 2 * NB), BF1...  54 us
    pallas_call x1, Pallas kernels, local(): pl.pallas_call(apply_shift, grid=(RD // ROWS,), out_shape=jax.ShapeDtypeS...  4.68 us

profile of v2, /device:TPU:1, one launch (start us, length us, event | category | flops | bytes accessed | tf_op | source)
XLA Modules:
  0.0 58.7 jit_solution(10356250775305669009)
XLA Ops:
  0.0 54.0 %gather_and_reduce.1 = (bf16[6144,256]{1,0:T(8,128)(2,1)S(1)}, bf16[256,512]{1,0:T(8,128)(2,1)S(1)}, bf16[6144,512]{1,0:T(8,128)(2,1)S(1)}) custom-call(s32[2]{0:T(128)} %offsets.1, bf16[2,8,6144]{2,1,0:T(8,128)(2,1)} %panels.1, bf16[6144,512]{1,0:T(8,128)(2,1)} %eig.1, f32[2,128,128]{2,1,0:T(8,128)} %tf.1), custom_call_target="tpu_custom_call" | custom-call | tf_op jit(solution)/shard_map/gather_and_reduce/pallas_call | solution.py:359
  54.0 4.7 %apply_shift.1 = bf16[6144,512]{1,0:T(8,128)(2,1)} custom-call(bf16[6144,256]{1,0:T(8,128)(2,1)S(1)} %get-tuple-element.8.HT, bf16[256,512]{1,0:T(8,128)(2,1)S(1)} %get-tuple-element.9.Y, bf16[6144,512]{1,0:T(8,128)(2,1)S(1)} %get-tuple-element.10.E), custom_call_target="tpu_custom_call" | custom-call | tf_op jit(solution)/shard_map/apply_shift/pallas_call | solution.py:400

commit v3 on v2

--- a/solution.py
+++ b/solution.py
@@ -20,9 +20,9 @@
 SLOTS = NX * NX
 HALF = RD // 2
 QUART = RD // 4
+NEAR_A = (0, 1, 4, 5, 6, 7, 10, 11, 12, 13, 14, 15, 18, 19)
 CHUNK = NX * OWN
-KT = 1536
-ORDER = (0, 1, 3, 2)
+NEAR = (0, 1, 3)
 
 
 def dot(a, b, dims=((1,), (0,)), precision=None):
@@ -35,7 +35,7 @@
 
 def gather_and_reduce(
     offsets, panels, eig, tf, HT, Y, E,
-    H, obuf, pbuf, tfbuf, T, ct, w1, c1, x1, z1, w0, c0, x0, z0, crow, C, ybuf,
+    H, obuf, pbuf, tfbuf, T, ct, w1, c1, x1, z1, wn, cn, xn, zn, wf, cf, xf, zf, crow, C, ybuf,
     local_sem, a_send, a_recv, b_send, b_recv,
     w_send, w_recv, z_send, z_recv, g_send, g_recv, c_send, c_recv, y_send, y_recv, f_send, f_recv,
 ):
@@ -102,6 +102,7 @@
         def __init__(self, p, lo, sems, first, second, turn):
             self.p, self.lo, self.sems = p, lo, sems
             self.first, self.second, self.turn = first, second, turn
+            self.got = set()
 
         def ref(self, d1, d2, piece=None):
             lo, n = (self.lo, HALF) if piece is None else (self.lo + piece * QUART, QUART)
@@ -110,55 +111,63 @@
         def put(self, ref, i, dev):
             send(ref, ref, self.sems[0].at[self.p, i], self.sems[1].at[self.p, i], dev)
 
-        def get(self, ref, i):
+        def get(self, i):
+            if i in self.got:
+                return
+            self.got.add(i)
+            if i < 2:
+                ref = self.ref((-1, 1)[i], 0)
+            elif i < 4:
+                ref = self.ref(2, 0, i - 2)
+            elif i < 12:
+                ref = self.ref((i - 4) // 2, (-1, 1)[i % 2])
+            else:
+                ref = self.ref((i - 12) // 2, 2, i % 2)
             recv(ref, self.sems[0].at[self.p, i], self.sems[1].at[self.p, i])
 
-        def send_own(self):
+        def line(self, d):
+            self.put(self.ref(d, 0), 4 + 2 * d, self.second(1))
+            self.put(self.ref(d, 0), 5 + 2 * d, self.second(-1))
+
+        def own(self):
             self.put(self.ref(0, 0), 0, self.first(1))
             self.put(self.ref(0, 0), 1, self.first(-1))
 
-        def recv_own(self):
-            self.get(self.ref(-1, 0), 0)
-            self.get(self.ref(1, 0), 1)
-
-        def send_far(self):
+        def own_line(self):
+            self.line(0)
+
+        def up(self):
+            self.get(0)
             self.put(self.ref(-1, 0, 0), 2, self.first(1))
+
+        def down(self):
+            self.get(1)
             self.put(self.ref(1, 0, 1), 3, self.first(-1))
 
-        def recv_far(self):
-            self.get(self.ref(2, 0, 0), 2)
-            self.get(self.ref(2, 0, 1), 3)
-
-        def send_line(self, d):
-            self.put(self.ref(d, 0), 4 + 2 * d, self.second(1))
-            self.put(self.ref(d, 0), 5 + 2 * d, self.second(-1))
-
-        def recv_line(self, d):
-            self.get(self.ref(d, -1), 4 + 2 * d)
-            self.get(self.ref(d, 1), 5 + 2 * d)
-
-        def send_far_line(self, d):
+        def low_line(self):
+            self.get(0)
+            self.line(3)
+
+        def high_line(self):
+            self.get(1)
+            self.line(1)
+
+        def far_line(self):
+            self.get(2)
+            self.get(3)
+            self.line(2)
+
+        def up_line(self, d):
+            self.get(4 + 2 * d)
             self.put(self.ref(d, -1, 0), 12 + 2 * d, self.second(1))
+
+        def down_line(self, d):
+            self.get(5 + 2 * d)
             self.put(self.ref(d, 1, 1), 13 + 2 * d, self.second(-1))
 
-        def recv_far_line(self, d):
-            self.get(self.ref(d, 2, 0), 12 + 2 * d)
-            self.get(self.ref(d, 2, 1), 13 + 2 * d)
-
-        def own_on(self):
-            self.recv_own()
-            self.send_far()
-            self.send_line(1)
-            self.send_line(3)
-
-        def line_on(self, *ds):
-            for d in ds:
-                self.recv_line(d)
-                self.send_far_line(d)
-
-        def far_on(self):
-            self.recv_far()
-            self.send_line(2)
+        def need(self, keys):
+            for i in keys:
+                self.get(i)
 
     halves = {
         p: (
@@ -173,58 +182,91 @@
     theirs = pl.ds(pl.multiple_of((1 - core) * KH, KH), KH)
     mine = pl.ds(pl.multiple_of(core * KH, KH), KH)
 
-    def products_one():
-        for t in range(RD // KT):
-            k = slice(t * KT, (t + 1) * KT)
-            h = H[1, :, :, k].reshape(NB, KT)
-            s = dot(h, E[k, :])
-            c = dot(h, H[0, slot, :, k], ((1,), (1,)))
-            if t:
-                s, c = s + w1[...], c + ct[...]
-            w1[...] = s
-            ct[...] = c
+    first_one = []
+
+    def products_one(half, lo, n):
+        half.need(range(20))
+        k = slice(lo, lo + n)
+        h = H[1, :, :, k].reshape(NB, n)
+        s = dot(h, E[k, :])
+        c = dot(h, H[0, slot, :, k], ((1,), (1,)))
+        w1[...] = s + w1[...] if first_one else s
+        ct[...] = c + ct[...] if first_one else c
+        first_one.append(lo)
+
+    def swap_one():
+        send(w1.at[:, theirs], c1, w_send.at[2], w_recv.at[2], sibling)
         crow[0] = ct[...].T
         for d in range(1, 16):
             send(crow.at[0], crow.at[d], g_send.at[d], g_recv.at[d], {"row": (row + d) % 16})
-        send(w1.at[:, theirs], c1, w_send.at[NX], w_recv.at[NX], sibling)
 
     def scatter_one():
-        recv(c1, w_send.at[NX], w_recv.at[NX])
+        recv(c1, w_send.at[2], w_recv.at[2])
         x1[...] = (w1[:, mine] + c1[...]).T.reshape(4, 64, NB)
         for d in (4, 3, 5, 2, 6, 1, 7):
             r = pl.multiple_of(((z + d) % NZ) * 8, 8)
-            send(x1.at[:, pl.ds(r, 8), :], z1.at[d], z_send.at[NX, d], z_recv.at[NX, d], at_z(d))
+            send(x1.at[:, pl.ds(r, 8), :], z1.at[d], z_send.at[2, d], z_recv.at[2, d], at_z(d))
 
     def collect_one():
         total = x1[:, pl.ds(pl.multiple_of(z * 8, 8), 8), :]
         for d in range(1, NZ):
-            recv(z1.at[d], z_send.at[NX, d], z_recv.at[NX, d])
+            recv(z1.at[d], z_send.at[2, d], z_recv.at[2, d])
             total = total + z1[d]
         return total.reshape(32, NB)
 
-    def products(k, lo, hi):
-        sx = (x + ORDER[k]) % NX
-        for t in range(lo // KT, hi // KT):
-            ks = slice(t * KT, (t + 1) * KT)
-            s = dot(H[0, pl.ds(sx * NX, NX), :, ks].reshape(CHUNK, KT), E[ks, :])
-            w0[k] = s + w0[k] if t else s
-
-    def swap(k):
-        send(w0.at[k, :, theirs], c0.at[k], w_send.at[k], w_recv.at[k], sibling)
-
-    def scatter(k):
-        recv(c0.at[k], w_send.at[k], w_recv.at[k])
-        s = w0[k, :, mine] + c0[k]
-        x0[k] = jnp.concatenate([s[:, g * 64 : g * 64 + 64] for g in range(4)], axis=0).T
+    first_near = []
+
+    def near(half, keys, lo, n):
+        half.need(keys)
+        k = slice(lo, lo + n)
+        h = [H[0, pl.ds(((x + d) % NX) * NX, NX), :, k].reshape(CHUNK, n) for d in NEAR]
+        s = dot(jnp.concatenate(h, axis=0), E[k, :])
+        wn[...] = s + wn[...] if first_near else s
+        first_near.append(lo)
+
+    def swap_near():
+        send(wn.at[:, theirs], cn, w_send.at[0], w_recv.at[0], sibling)
+
+    def scatter_near():
+        recv(cn, w_send.at[0], w_recv.at[0])
+        s = jnp.concatenate([wn[:, mine] + cn[...], jnp.zeros((CHUNK, KH), F32)], axis=0)
+        xn[...] = s.T.reshape(4, 64, NB)
         for d in (4, 3, 5, 2, 6, 1, 7):
             r = pl.multiple_of(((z + d) % NZ) * 8, 8)
-            send(x0.at[k, pl.ds(r, 8), :], z0.at[k, d], z_send.at[k, d], z_recv.at[k, d], at_z(d))
-
-    def collect(k):
-        total = x0[k, pl.ds(pl.multiple_of(z * 8, 8), 8), :]
+            send(xn.at[:, pl.ds(r, 8), :], zn.at[d], z_send.at[0, d], z_recv.at[0, d], at_z(d))
+
+    def collect_near():
+        total = xn[:, pl.ds(pl.multiple_of(z * 8, 8), 8), :]
         for d in range(1, NZ):
-            recv(z0.at[k, d], z_send.at[k, d], z_recv.at[k, d])
-            total = total + z0[k, d]
+            recv(zn.at[d], z_send.at[0, d], z_recv.at[0, d])
+            total = total + zn[d]
+        return total.reshape(32, NB)[:, : 3 * CHUNK]
+
+    first_far = []
+
+    def far(half, keys, lo, n):
+        half.need(keys)
+        k = slice(lo, lo + n)
+        s = dot(H[0, pl.ds(((x + 2) % NX) * NX, NX), :, k].reshape(CHUNK, n), E[k, :])
+        wf[...] = s + wf[...] if first_far else s
+        first_far.append(lo)
+
+    def swap_far():
+        send(wf.at[:, theirs], cf, w_send.at[1], w_recv.at[1], sibling)
+
+    def scatter_far():
+        recv(cf, w_send.at[1], w_recv.at[1])
+        s = wf[:, mine] + cf[...]
+        xf[...] = jnp.concatenate([s[:, g * 64 : g * 64 + 64] for g in range(4)], axis=0).T
+        for d in (4, 3, 5, 2, 6, 1, 7):
+            r = pl.multiple_of(((z + d) % NZ) * 8, 8)
+            send(xf.at[pl.ds(r, 8), :], zf.at[d], z_send.at[1, d], z_recv.at[1, d], at_z(d))
+
+    def collect_far():
+        total = xf[pl.ds(pl.multiple_of(z * 8, 8), 8), :]
+        for d in range(1, NZ):
+            recv(zf.at[d], z_send.at[1, d], z_recv.at[1, d])
+            total = total + zf[d]
         return jnp.concatenate([total[:, g * CHUNK : (g + 1) * CHUNK] for g in range(4)], axis=0)
 
     def cross_sum():
@@ -270,72 +312,100 @@
         for r in range(0, RD, 512):
             HT[r : r + 512, p * NB : (p + 1) * NB] = H[p, :, :, r : r + 512].reshape(NB, 512).T
 
-    a1.send_own()
-    b1.send_own()
-    a1.send_line(0)
-    b1.send_line(0)
-    load_tf.wait()
-    for p in range(2):
+    def upper_factors():
+        load_tf.wait()
         tri = lax.broadcasted_iota(jnp.int32, (NB, NB), 0) <= lax.broadcasted_iota(jnp.int32, (NB, NB), 1)
-        T[p] = by_place(by_place(jnp.where(tri, tfbuf[p], 0.0)).T)
-    a0.send_own()
-    b0.send_own()
-    a0.send_line(0)
-    b0.send_line(0)
-    a1.own_on()
-    b1.own_on()
-    a1.line_on(0)
-    b1.line_on(0)
-    a1.far_on()
-    b1.far_on()
-    a0.own_on()
-    b0.own_on()
-    a1.line_on(1, 3)
-    b1.line_on(1, 3)
-    a0.line_on(0)
-    b0.line_on(0)
-    a1.line_on(2)
-    b1.line_on(2)
-    a0.far_on()
-    b0.far_on()
-    a0.line_on(1, 3)
-    b0.line_on(1, 3)
+        for p in range(2):
+            T[p] = by_place(by_place(jnp.where(tri, tfbuf[p], 0.0)).T)
+
+    b1.own()
+    b0.own()
+    a1.own()
+    a0.own()
+    b1.own_line()
+    a0.own_line()
+    upper_factors()
+    b1.high_line()
+    b1.down()
+    b1.up()
+    a1.up()
+    a1.own_line()
+    a1.down()
+    a0.up()
+    a1.high_line()
+    b1.low_line()
+    b0.down()
+    b1.down_line(0)
+    b0.up()
+    a1.low_line()
+    b1.far_line()
+    b0.high_line()
+    a1.far_line()
+    b1.up_line(0)
+    a0.low_line()
+    a0.high_line()
+    a1.down_line(0)
+    b1.up_line(1)
+    a0.down()
+    b1.down_line(1)
+    b1.up_line(3)
+    b1.down_line(2)
+    b1.up_line(2)
+    a0.down_line(0)
+    a1.up_line(1)
+    b1.down_line(3)
+    a1.down_line(3)
+    b0.low_line()
+    a1.up_line(0)
+    a1.down_line(1)
+    a1.down_line(2)
+    a1.up_line(3)
+    b0.own_line()
+    b0.far_line()
+    b0.down_line(1)
+    b0.up_line(1)
+    a1.up_line(2)
+    a0.far_line()
+    a0.up_line(0)
+    a0.down_line(1)
+    a0.down_line(3)
     load_eig.wait()
-    for d in range(NX):
-        a1.recv_far_line(d)
-        b1.recv_far_line(d)
-    products_one()
-    a0.line_on(2)
-    b0.line_on(2)
+    products_one(b1, HALF + QUART, QUART)
+    products_one(b1, HALF, QUART)
+    b0.down_line(3)
+    b0.up_line(0)
+    b0.up_line(3)
+    a0.up_line(3)
+    a0.up_line(1)
+    b0.down_line(0)
+    products_one(a1, 0, QUART)
+    b0.down_line(2)
+    b0.up_line(2)
+    a0.down_line(2)
+    products_one(a1, QUART, QUART)
+    a0.up_line(2)
+    near(b0, range(12), HALF, QUART)
+    swap_one()
+    near(a0, NEAR_A, QUART, QUART)
+    near(a0, NEAR_A, 0, QUART)
+    near(b0, range(12), HALF + QUART, QUART)
+    swap_near()
     scatter_one()
-    a0.recv_far_line(0)
-    products(0, 0, RD)
-    swap(0)
-    a0.recv_far_line(1)
-    products(1, 0, RD)
-    swap(1)
+    far(a0, range(20), 0, HALF)
+    scatter_near()
+    far(b0, range(20), HALF, HALF)
+    swap_far()
     cross_sum()
-    a0.recv_far_line(3)
-    products(2, 0, RD)
-    swap(2)
-    scatter(0)
-    scatter(1)
-    a0.recv_far_line(2)
-    products(3, 0, HALF)
-    for d in range(NX):
-        b0.recv_far_line(d)
-    products(3, HALF, RD)
-    swap(3)
-    scatter(2)
+    scatter_far()
     y1 = dot(collect_one(), T[1], precision=HIGH).astype(BF16)
     spread(1, y1)
-    scatter(3)
     turn(1)
     turn(0)
     cross = cross_recv()
     shift = dot(y1.astype(F32), cross, ((1,), (1,)), precision=HIGH)
-    parts = {ORDER[k]: collect(k) for k in range(NX)}
-    total = pltpu.roll(jnp.concatenate([parts[d] for d in range(NX)], axis=1), x * CHUNK, 1)
+    near_sum = collect_near()
+    total = [near_sum[:, : 2 * CHUNK], collect_far(), near_sum[:, 2 * CHUNK :]]
+    total = pltpu.roll(jnp.concatenate(total, axis=1), x * CHUNK, 1)
     spread(0, dot(total - shift, T[0], precision=HIGH).astype(BF16))
     pass_on(1)
     finish(1)
@@ -345,12 +415,18 @@
         cp.wait_send()
 
 
-ROWS = 1024
-
-
-def apply_shift(HT, Y, E, out):
-    rows = pl.ds(pl.multiple_of(pl.program_id(0) * ROWS, ROWS), ROWS)
-    out[...] = (E[rows, :].astype(F32) - dot(HT[rows, :], Y[...])).astype(BF16)
+ROWS = 512
+
+
+def apply_shift(HT, Y, E, out, done, sems):
+    copies = []
+    for i in range(RD // ROWS):
+        rows = slice(i * ROWS, (i + 1) * ROWS)
+        done[rows, :] = (E[rows, :].astype(F32) - dot(HT[rows, :], Y[...])).astype(BF16)
+        copies.append(pltpu.make_async_copy(done.at[rows, :], out.at[rows, :], sems.at[i]))
+        copies[-1].start()
+    for cp in copies:
+        cp.wait()
 
 
 def local(eigvecs, panels, tfactors, offsets):
@@ -376,17 +452,21 @@
             pltpu.VMEM((NB, KH), F32),
             pltpu.VMEM((4, 64, NB), F32),
             pltpu.VMEM((NZ, 4, 8, NB), F32),
-            pltpu.VMEM((NX, CHUNK, KD), F32),
-            pltpu.VMEM((NX, CHUNK, KH), F32),
-            pltpu.VMEM((NX, 64, 128), F32),
-            pltpu.VMEM((NX, NZ, 8, 128), F32),
+            pltpu.VMEM((3 * CHUNK, KD), F32),
+            pltpu.VMEM((3 * CHUNK, KH), F32),
+            pltpu.VMEM((4, 64, NB), F32),
+            pltpu.VMEM((NZ, 4, 8, NB), F32),
+            pltpu.VMEM((CHUNK, KD), F32),
+            pltpu.VMEM((CHUNK, KH), F32),
+            pltpu.VMEM((64, 128), F32),
+            pltpu.VMEM((NZ, 8, 128), F32),
             pltpu.VMEM((16, OWN, NB), F32),
             pltpu.VMEM((SLOTS, OWN, NB), F32),
             pltpu.VMEM((2, 16, 32, NB), BF16),
             dma((4,)),
             dma((2, 20)), dma((2, 20)), dma((2, 20)), dma((2, 20)),
-            dma((NX + 1,)), dma((NX + 1,)),
-            dma((NX + 1, NZ)), dma((NX + 1, NZ)),
+            dma((3,)), dma((3,)),
+            dma((3, NZ)), dma((3, NZ)),
             dma((16,)), dma((16,)), dma((16,)), dma((16,)),
             dma((2, NZ)), dma((2, NZ)),
             dma((2, NZ)), dma((2, NZ)),
@@ -399,10 +479,10 @@
     whole = pl.BlockSpec(memory_space=pltpu.VMEM)
     return pl.pallas_call(
         apply_shift,
-        grid=(RD // ROWS,),
         out_shape=jax.ShapeDtypeStruct((RD, KD), BF16),
         in_specs=[whole, whole, whole],
-        out_specs=pl.BlockSpec((ROWS, KD), lambda i: (i, 0)),
+        out_specs=hbm,
+        scratch_shapes=[pltpu.VMEM((RD, KD), BF16), dma((RD // ROWS,))],
         compiler_params=pltpu.CompilerParams(vmem_limit_bytes=40 * 1024 * 1024),
         name="apply_shift",
     )(HT, Y, E)

time: 58.8 us -> 53.6 us (0.912)
  Pallas kernels: 58.7 us -> 53.5 us
    pallas_call x1, Pallas kernels: 54 us -> 50.4 us  [local(): pl.pallas_call(gather_and_reduce, out_shape=[pltpu.VMEM((RD, 2 * NB), BF1...]
    pallas_call x1, Pallas kernels: 4.68 us -> 3.05 us  [local(): pl.pallas_call(apply_shift, out_shape=jax.ShapeDtypeStruct((RD, KD), BF16...]
where the time goes in v3:
time: 53.6 us; the launch traced here: 53.5 us
  Pallas kernels  53.5 us (100%)
    pallas_call x1, Pallas kernels, local(): pl.pallas_call(gather_and_reduce, out_shape=[pltpu.VMEM((RD, 2 * NB), BF1...  50.4 us
    pallas_call x1, Pallas kernels, local(): pl.pallas_call(apply_shift, out_shape=jax.ShapeDtypeStruct((RD, KD), BF16...  3.05 us

profile of v3, /device:TPU:1, one launch (start us, length us, event | category | flops | bytes accessed | tf_op | source)
XLA Modules:
  0.0 53.5 jit_solution(15048324803370504922)
XLA Ops:
  0.0 50.4 %gather_and_reduce.1 = (bf16[6144,256]{1,0:T(8,128)(2,1)S(1)}, bf16[256,512]{1,0:T(8,128)(2,1)S(1)}, bf16[6144,512]{1,0:T(8,128)(2,1)S(1)}) custom-call(s32[2]{0:T(128)} %offsets.1, bf16[2,8,6144]{2,1,0:T(8,128)(2,1)} %panels.1, bf16[6144,512]{1,0:T(8,128)(2,1)} %eig.1, f32[2,128,128]{2,1,0:T(8,128)} %tf.1), custom_call_target="tpu_custom_call" | custom-call | tf_op jit(solution)/shard_map/gather_and_reduce/pallas_call | solution.py:435
  50.4 3.1 %apply_shift.1 = bf16[6144,512]{1,0:T(8,128)(2,1)} custom-call(bf16[6144,256]{1,0:T(8,128)(2,1)S(1)} %get-tuple-element.8.HT, bf16[256,512]{1,0:T(8,128)(2,1)S(1)} %get-tuple-element.9.Y, bf16[6144,512]{1,0:T(8,128)(2,1)S(1)} %get-tuple-element.10.E), custom_call_target="tpu_custom_call" | custom-call | tf_op jit(solution)/shard_map/apply_shift/pallas_call | solution.py:480

commit v4 on v3

--- a/solution.py
+++ b/solution.py
@@ -20,9 +20,6 @@
 SLOTS = NX * NX
 HALF = RD // 2
 QUART = RD // 4
-NEAR_A = (0, 1, 4, 5, 6, 7, 10, 11, 12, 13, 14, 15, 18, 19)
-CHUNK = NX * OWN
-NEAR = (0, 1, 3)
 
 
 def dot(a, b, dims=((1,), (0,)), precision=None):
@@ -35,7 +32,7 @@
 
 def gather_and_reduce(
     offsets, panels, eig, tf, HT, Y, E,
-    H, obuf, pbuf, tfbuf, T, ct, w1, c1, x1, z1, wn, cn, xn, zn, wf, cf, xf, zf, crow, C, ybuf,
+    H, obuf, pbuf, tfbuf, T, ct, w1, c1, x1, z1, w0, c0, x0, z0, crow, C, ybuf,
     local_sem, a_send, a_recv, b_send, b_recv,
     w_send, w_recv, z_send, z_recv, g_send, g_recv, c_send, c_recv, y_send, y_recv, f_send, f_recv,
 ):
@@ -92,6 +89,11 @@
         cp = pltpu.make_async_remote_copy(src, dst, send_sem, recv_sem, device_id=dev, device_id_type=MESH)
         cp.start()
         sent.append(cp)
+
+    def settle():
+        for cp in sent:
+            cp.wait_send()
+        sent.clear()
 
     def recv(ref, send_sem, recv_sem):
         pltpu.make_async_remote_copy(
@@ -194,80 +196,37 @@
         ct[...] = c + ct[...] if first_one else c
         first_one.append(lo)
 
-    def swap_one():
-        send(w1.at[:, theirs], c1, w_send.at[2], w_recv.at[2], sibling)
+    def send_cross():
         crow[0] = ct[...].T
         for d in range(1, 16):
             send(crow.at[0], crow.at[d], g_send.at[d], g_recv.at[d], {"row": (row + d) % 16})
 
-    def scatter_one():
-        recv(c1, w_send.at[2], w_recv.at[2])
-        x1[...] = (w1[:, mine] + c1[...]).T.reshape(4, 64, NB)
+    first_zero = []
+
+    def products_zero(half, lo, n):
+        half.need(range(20))
+        k = slice(lo, lo + n)
+        w = dot(H[0, :, :, k].reshape(NB, n), E[k, :])
+        w0[...] = w + w0[...] if first_zero else w
+        first_zero.append(lo)
+
+    def swap(i, w, c):
+        send(w.at[:, theirs], c, w_send.at[i], w_recv.at[i], sibling)
+
+    def scatter(i, w, c, xs, zs):
+        recv(c, w_send.at[i], w_recv.at[i])
+        s = (w[:, mine] + c[...]).T.reshape(4, NZ, 8, NB)
+        for g in range(4):
+            xs[:, g] = s[g]
         for d in (4, 3, 5, 2, 6, 1, 7):
-            r = pl.multiple_of(((z + d) % NZ) * 8, 8)
-            send(x1.at[:, pl.ds(r, 8), :], z1.at[d], z_send.at[2, d], z_recv.at[2, d], at_z(d))
-
-    def collect_one():
-        total = x1[:, pl.ds(pl.multiple_of(z * 8, 8), 8), :]
+            send(xs.at[(z + d) % NZ], zs.at[d], z_send.at[i, d], z_recv.at[i, d], at_z(d))
+
+    def collect(i, xs, zs):
+        total = xs[z]
         for d in range(1, NZ):
-            recv(z1.at[d], z_send.at[2, d], z_recv.at[2, d])
-            total = total + z1[d]
+            recv(zs.at[d], z_send.at[i, d], z_recv.at[i, d])
+            total = total + zs[d]
         return total.reshape(32, NB)
-
-    first_near = []
-
-    def near(half, keys, lo, n):
-        half.need(keys)
-        k = slice(lo, lo + n)
-        h = [H[0, pl.ds(((x + d) % NX) * NX, NX), :, k].reshape(CHUNK, n) for d in NEAR]
-        s = dot(jnp.concatenate(h, axis=0), E[k, :])
-        wn[...] = s + wn[...] if first_near else s
-        first_near.append(lo)
-
-    def swap_near():
-        send(wn.at[:, theirs], cn, w_send.at[0], w_recv.at[0], sibling)
-
-    def scatter_near():
-        recv(cn, w_send.at[0], w_recv.at[0])
-        s = jnp.concatenate([wn[:, mine] + cn[...], jnp.zeros((CHUNK, KH), F32)], axis=0)
-        xn[...] = s.T.reshape(4, 64, NB)
-        for d in (4, 3, 5, 2, 6, 1, 7):
-            r = pl.multiple_of(((z + d) % NZ) * 8, 8)
-            send(xn.at[:, pl.ds(r, 8), :], zn.at[d], z_send.at[0, d], z_recv.at[0, d], at_z(d))
-
-    def collect_near():
-        total = xn[:, pl.ds(pl.multiple_of(z * 8, 8), 8), :]
-        for d in range(1, NZ):
-            recv(zn.at[d], z_send.at[0, d], z_recv.at[0, d])
-            total = total + zn[d]
-        return total.reshape(32, NB)[:, : 3 * CHUNK]
-
-    first_far = []
-
-    def far(half, keys, lo, n):
-        half.need(keys)
-        k = slice(lo, lo + n)
-        s = dot(H[0, pl.ds(((x + 2) % NX) * NX, NX), :, k].reshape(CHUNK, n), E[k, :])
-        wf[...] = s + wf[...] if first_far else s
-        first_far.append(lo)
-
-    def swap_far():
-        send(wf.at[:, theirs], cf, w_send.at[1], w_recv.at[1], sibling)
-
-    def scatter_far():
-        recv(cf, w_send.at[1], w_recv.at[1])
-        s = wf[:, mine] + cf[...]
-        xf[...] = jnp.concatenate([s[:, g * 64 : g * 64 + 64] for g in range(4)], axis=0).T
-        for d in (4, 3, 5, 2, 6, 1, 7):
-            r = pl.multiple_of(((z + d) % NZ) * 8, 8)
-            send(xf.at[pl.ds(r, 8), :], zf.at[d], z_send.at[1, d], z_recv.at[1, d], at_z(d))
-
-    def collect_far():
-        total = xf[pl.ds(pl.multiple_of(z * 8, 8), 8), :]
-        for d in range(1, NZ):
-            recv(zf.at[d], z_send.at[1, d], z_recv.at[1, d])
-            total = total + zf[d]
-        return jnp.concatenate([total[:, g * CHUNK : (g + 1) * CHUNK] for g in range(4)], axis=0)
 
     def cross_sum():
         total = crow[0]
@@ -319,100 +278,91 @@
             T[p] = by_place(by_place(jnp.where(tri, tfbuf[p], 0.0)).T)
 
     b1.own()
+    a1.own_line()
+    a1.own()
     b0.own()
-    a1.own()
+    b0.own_line()
     a0.own()
-    b1.own_line()
     a0.own_line()
     upper_factors()
+    a1.up()
+    a1.down()
+    b1.up()
+    a1.low_line()
     b1.high_line()
     b1.down()
-    b1.up()
-    a1.up()
-    a1.own_line()
-    a1.down()
+    b1.own_line()
+    a1.high_line()
+    b0.low_line()
+    b0.up()
     a0.up()
-    a1.high_line()
+    a1.far_line()
+    a1.up_line(0)
+    a1.down_line(0)
+    a0.down()
     b1.low_line()
+    b1.far_line()
+    a0.high_line()
     b0.down()
+    a0.down_line(0)
+    a1.down_line(1)
+    b1.up_line(0)
+    a1.down_line(3)
+    a1.up_line(1)
+    b1.down_line(1)
+    b0.high_line()
     b1.down_line(0)
-    b0.up()
-    a1.low_line()
-    b1.far_line()
-    b0.high_line()
-    a1.far_line()
-    b1.up_line(0)
+    a1.up_line(2)
+    b1.up_line(3)
+    b0.up_line(0)
+    a1.down_line(2)
+    a0.up_line(0)
+    a1.up_line(3)
     a0.low_line()
-    a0.high_line()
-    a1.down_line(0)
     b1.up_line(1)
-    a0.down()
-    b1.down_line(1)
-    b1.up_line(3)
+    a0.far_line()
     b1.down_line(2)
+    b0.far_line()
+    a0.down_line(1)
+    b1.down_line(3)
     b1.up_line(2)
-    a0.down_line(0)
-    a1.up_line(1)
-    b1.down_line(3)
-    a1.down_line(3)
-    b0.low_line()
-    a1.up_line(0)
-    a1.down_line(1)
-    a1.down_line(2)
-    a1.up_line(3)
-    b0.own_line()
-    b0.far_line()
     b0.down_line(1)
+    b0.down_line(0)
+    b0.up_line(3)
     b0.up_line(1)
-    a1.up_line(2)
-    a0.far_line()
-    a0.up_line(0)
-    a0.down_line(1)
-    a0.down_line(3)
+    b0.down_line(3)
+    a0.up_line(1)
     load_eig.wait()
-    products_one(b1, HALF + QUART, QUART)
-    products_one(b1, HALF, QUART)
-    b0.down_line(3)
-    b0.up_line(0)
-    b0.up_line(3)
-    a0.up_line(3)
-    a0.up_line(1)
-    b0.down_line(0)
-    products_one(a1, 0, QUART)
+    products_one(a1, 0, HALF)
     b0.down_line(2)
     b0.up_line(2)
+    a0.down_line(3)
+    a0.up_line(3)
+    a0.up_line(2)
     a0.down_line(2)
-    products_one(a1, QUART, QUART)
-    a0.up_line(2)
-    near(b0, range(12), HALF, QUART)
-    swap_one()
-    near(a0, NEAR_A, QUART, QUART)
-    near(a0, NEAR_A, 0, QUART)
-    near(b0, range(12), HALF + QUART, QUART)
-    swap_near()
-    scatter_one()
-    far(a0, range(20), 0, HALF)
-    scatter_near()
-    far(b0, range(20), HALF, HALF)
-    swap_far()
+    products_one(b1, HALF, HALF)
+    send_cross()
+    swap(1, w1, c1)
+    products_zero(b0, HALF, HALF)
+    scatter(1, w1, c1, x1, z1)
+    products_zero(a0, 0, HALF)
+    swap(0, w0, c0)
+    scatter(0, w0, c0, x0, z0)
     cross_sum()
-    scatter_far()
-    y1 = dot(collect_one(), T[1], precision=HIGH).astype(BF16)
+    y1 = dot(collect(1, x1, z1), T[1], precision=HIGH).astype(BF16)
     spread(1, y1)
     turn(1)
     turn(0)
     cross = cross_recv()
     shift = dot(y1.astype(F32), cross, ((1,), (1,)), precision=HIGH)
-    near_sum = collect_near()
-    total = [near_sum[:, : 2 * CHUNK], collect_far(), near_sum[:, 2 * CHUNK :]]
-    total = pltpu.roll(jnp.concatenate(total, axis=1), x * CHUNK, 1)
+    total = collect(0, x0, z0)
     spread(0, dot(total - shift, T[0], precision=HIGH).astype(BF16))
     pass_on(1)
     finish(1)
+    settle()
     pass_on(0)
     finish(0)
-    for cp in sent:
-        cp.wait_send()
+    settle()
 
 
 ROWS = 512
@@ -450,23 +400,19 @@
             pltpu.VMEM((NB, OWN), F32),
             pltpu.VMEM((NB, KD), F32),
             pltpu.VMEM((NB, KH), F32),
-            pltpu.VMEM((4, 64, NB), F32),
             pltpu.VMEM((NZ, 4, 8, NB), F32),
-            pltpu.VMEM((3 * CHUNK, KD), F32),
-            pltpu.VMEM((3 * CHUNK, KH), F32),
-            pltpu.VMEM((4, 64, NB), F32),
             pltpu.VMEM((NZ, 4, 8, NB), F32),
-            pltpu.VMEM((CHUNK, KD), F32),
-            pltpu.VMEM((CHUNK, KH), F32),
-            pltpu.VMEM((64, 128), F32),
-            pltpu.VMEM((NZ, 8, 128), F32),
+            pltpu.VMEM((NB, KD), F32),
+            pltpu.VMEM((NB, KH), F32),
+            pltpu.VMEM((NZ, 4, 8, NB), F32),
+            pltpu.VMEM((NZ, 4, 8, NB), F32),
             pltpu.VMEM((16, OWN, NB), F32),
             pltpu.VMEM((SLOTS, OWN, NB), F32),
             pltpu.VMEM((2, 16, 32, NB), BF16),
             dma((4,)),
             dma((2, 20)), dma((2, 20)), dma((2, 20)), dma((2, 20)),
-            dma((3,)), dma((3,)),
-            dma((3, NZ)), dma((3, NZ)),
+            dma((2,)), dma((2,)),
+            dma((2, NZ)), dma((2, NZ)),
             dma((16,)), dma((16,)), dma((16,)), dma((16,)),
             dma((2, NZ)), dma((2, NZ)),
             dma((2, NZ)), dma((2, NZ)),

time: 53.6 us -> 51.8 us (0.966)
  Pallas kernels: 53.5 us -> 51.7 us
    pallas_call x1, Pallas kernels: 50.4 us -> 48.7 us  [local(): pl.pallas_call(gather_and_reduce, out_shape=[pltpu.VMEM((RD, 2 * NB), BF1...]
where the time goes in v4:
time: 51.8 us
  Pallas kernels  51.7 us (100%)
    pallas_call x1, Pallas kernels, local(): pl.pallas_call(gather_and_reduce, out_shape=[pltpu.VMEM((RD, 2 * NB), BF1...  48.7 us
    pallas_call x1, Pallas kernels, local(): pl.pallas_call(apply_shift, out_shape=jax.ShapeDtypeStruct((RD, KD), BF16...  3.05 us

profile of v4, /device:TPU:1, one launch (start us, length us, event | category | flops | bytes accessed | tf_op | source)
XLA Modules:
  0.0 51.8 jit_solution(6163918820343228767)
XLA Ops:
  0.0 48.7 %gather_and_reduce.1 = (bf16[6144,256]{1,0:T(8,128)(2,1)S(1)}, bf16[256,512]{1,0:T(8,128)(2,1)S(1)}, bf16[6144,512]{1,0:T(8,128)(2,1)S(1)}) custom-call(s32[2]{0:T(128)} %offsets.1, bf16[2,8,6144]{2,1,0:T(8,128)(2,1)} %panels.1, bf16[6144,512]{1,0:T(8,128)(2,1)} %eig.1, f32[2,128,128]{2,1,0:T(8,128)} %tf.1), custom_call_target="tpu_custom_call" | custom-call | tf_op jit(solution)/shard_map/gather_and_reduce/pallas_call | solution.py:385
  48.7 3.1 %apply_shift.1 = bf16[6144,512]{1,0:T(8,128)(2,1)} custom-call(bf16[6144,256]{1,0:T(8,128)(2,1)S(1)} %get-tuple-element.8.HT, bf16[256,512]{1,0:T(8,128)(2,1)S(1)} %get-tuple-element.9.Y, bf16[6144,512]{1,0:T(8,128)(2,1)S(1)} %get-tuple-element.10.E), custom_call_target="tpu_custom_call" | custom-call | tf_op jit(solution)/shard_map/apply_shift/pallas_call | solution.py:426

commit v5 on v4

--- a/solution.py
+++ b/solution.py
@@ -18,6 +18,7 @@
 NZ = 8
 OWN = 8
 SLOTS = NX * NX
+FAR = (4,)
 HALF = RD // 2
 QUART = RD // 4
 
@@ -47,8 +48,8 @@
     def at_y(d):
         return {"col": ((y + d) % NX) * NX + x}
 
-    def at_z(d):
-        return {"row": ((z + d) % NZ) * 2 + core}
+    def at_z(d, c=core):
+        return {"row": ((z + d) % NZ) * 2 + c}
 
     sibling = {"row": z * 2 + (1 - core)}
 
@@ -248,13 +249,16 @@
         ybuf[p, core * NZ + z] = value
         for d in (4, 3, 5, 2, 6, 1, 7):
             send(ref, ref, y_send.at[p, d], y_recv.at[p, d], at_z(d))
+            if d in FAR:
+                send(ref, ref, f_send.at[p, d], f_recv.at[p, d], at_z(d, 1 - core))
         send(ref, ref, f_send.at[p, 0], f_recv.at[p, 0], sibling)
 
     def pass_on(p):
         for d in (1, 7, 2, 6, 3, 5, 4):
             ref = ybuf.at[p, core * NZ + (z + NZ - d) % NZ]
             recv(ref, y_send.at[p, d], y_recv.at[p, d])
-            send(ref, ref, f_send.at[p, d], f_recv.at[p, d], sibling)
+            if d not in FAR:
+                send(ref, ref, f_send.at[p, d], f_recv.at[p, d], sibling)
 
     def place(p, c):
         v = [ybuf[p, c * NZ + i].astype(F32) for i in range(NZ)]
@@ -277,75 +281,75 @@
         for p in range(2):
             T[p] = by_place(by_place(jnp.where(tri, tfbuf[p], 0.0)).T)
 
+    a1.own()
     b1.own()
+    a0.own()
+    b0.own_line()
     a1.own_line()
-    a1.own()
     b0.own()
-    b0.own_line()
-    a0.own()
+    b1.own_line()
+    upper_factors()
+    b1.low_line()
+    b1.up()
+    b1.down()
     a0.own_line()
-    upper_factors()
     a1.up()
+    b1.high_line()
     a1.down()
-    b1.up()
     a1.low_line()
-    b1.high_line()
-    b1.down()
-    b1.own_line()
+    a1.up_line(0)
+    a0.up()
+    a0.down()
     a1.high_line()
+    a0.high_line()
+    b1.far_line()
+    a0.low_line()
+    b0.high_line()
+    b1.up_line(0)
+    b1.down_line(3)
+    b1.up_line(3)
     b0.low_line()
+    b0.down()
     b0.up()
-    a0.up()
+    b1.down_line(1)
     a1.far_line()
-    a1.up_line(0)
+    a0.far_line()
+    a1.up_line(3)
+    a1.down_line(3)
+    a1.down_line(1)
     a1.down_line(0)
-    a0.down()
-    b1.low_line()
-    b1.far_line()
-    a0.high_line()
-    b0.down()
+    a0.up_line(0)
+    b1.down_line(2)
+    b1.up_line(1)
+    b1.up_line(2)
+    b1.down_line(0)
+    a1.up_line(1)
+    b0.far_line()
+    b0.up_line(0)
+    a1.up_line(2)
+    b0.down_line(0)
+    a1.down_line(2)
+    a0.down_line(1)
+    a0.up_line(1)
+    b0.up_line(3)
+    b0.down_line(1)
+    a0.up_line(3)
+    a0.down_line(3)
+    b0.down_line(3)
+    a0.up_line(2)
+    b0.up_line(1)
     a0.down_line(0)
-    a1.down_line(1)
-    b1.up_line(0)
-    a1.down_line(3)
-    a1.up_line(1)
-    b1.down_line(1)
-    b0.high_line()
-    b1.down_line(0)
-    a1.up_line(2)
-    b1.up_line(3)
-    b0.up_line(0)
-    a1.down_line(2)
-    a0.up_line(0)
-    a1.up_line(3)
-    a0.low_line()
-    b1.up_line(1)
-    a0.far_line()
-    b1.down_line(2)
-    b0.far_line()
-    a0.down_line(1)
-    b1.down_line(3)
-    b1.up_line(2)
-    b0.down_line(1)
-    b0.down_line(0)
-    b0.up_line(3)
-    b0.up_line(1)
-    b0.down_line(3)
-    a0.up_line(1)
+    a0.down_line(2)
     load_eig.wait()
-    products_one(a1, 0, HALF)
+    products_one(b1, HALF, HALF)
     b0.down_line(2)
     b0.up_line(2)
-    a0.down_line(3)
-    a0.up_line(3)
-    a0.up_line(2)
-    a0.down_line(2)
-    products_one(b1, HALF, HALF)
+    products_one(a1, 0, HALF)
     send_cross()
     swap(1, w1, c1)
+    products_zero(a0, 0, HALF)
+    scatter(1, w1, c1, x1, z1)
     products_zero(b0, HALF, HALF)
-    scatter(1, w1, c1, x1, z1)
-    products_zero(a0, 0, HALF)
     swap(0, w0, c0)
     scatter(0, w0, c0, x0, z0)
     cross_sum()

time: 51.8 us -> 51.2 us (0.988)
  Pallas kernels: 51.7 us -> 51.1 us
    pallas_call x1, Pallas kernels: 48.7 us -> 48.1 us  [local(): pl.pallas_call(gather_and_reduce, out_shape=[pltpu.VMEM((RD, 2 * NB), BF1...]
where the time goes in v5:
time: 51.2 us; the launch traced here: 51.1 us
  Pallas kernels  51.1 us (100%)
    pallas_call x1, Pallas kernels, local(): pl.pallas_call(gather_and_reduce, out_shape=[pltpu.VMEM((RD, 2 * NB), BF1...  48.1 us
    pallas_call x1, Pallas kernels, local(): pl.pallas_call(apply_shift, out_shape=jax.ShapeDtypeStruct((RD, KD), BF16...  3.05 us

profile of v5, /device:TPU:1, one launch (start us, length us, event | category | flops | bytes accessed | tf_op | source)
XLA Modules:
  0.0 51.1 jit_solution(13807534744624783278)
XLA Ops:
  0.0 48.1 %gather_and_reduce.1 = (bf16[6144,256]{1,0:T(8,128)(2,1)S(1)}, bf16[256,512]{1,0:T(8,128)(2,1)S(1)}, bf16[6144,512]{1,0:T(8,128)(2,1)S(1)}) custom-call(s32[2]{0:T(128)} %offsets.1, bf16[2,8,6144]{2,1,0:T(8,128)(2,1)} %panels.1, bf16[6144,512]{1,0:T(8,128)(2,1)} %eig.1, f32[2,128,128]{2,1,0:T(8,128)} %tf.1), custom_call_target="tpu_custom_call" | custom-call | tf_op jit(solution)/shard_map/gather_and_reduce/pallas_call | solution.py:389
  48.1 3.1 %apply_shift.1 = bf16[6144,512]{1,0:T(8,128)(2,1)} custom-call(bf16[6144,256]{1,0:T(8,128)(2,1)S(1)} %get-tuple-element.8.HT, bf16[256,512]{1,0:T(8,128)(2,1)S(1)} %get-tuple-element.9.Y, bf16[6144,512]{1,0:T(8,128)(2,1)S(1)} %get-tuple-element.10.E), custom_call_target="tpu_custom_call" | custom-call | tf_op jit(solution)/shard_map/apply_shift/pallas_call | solution.py:430

commit v6 on v5

--- a/solution.py
+++ b/solution.py
@@ -345,8 +345,8 @@
     b0.down_line(2)
     b0.up_line(2)
     products_one(a1, 0, HALF)
+    swap(1, w1, c1)
     send_cross()
-    swap(1, w1, c1)
     products_zero(a0, 0, HALF)
     scatter(1, w1, c1, x1, z1)
     products_zero(b0, HALF, HALF)

time: 51.2 us -> 51.2 us (level)
  no operation moved by 1% of the time
where the time goes in v6:
time: 51.2 us; the launch traced here: 51.1 us
  Pallas kernels  51.1 us (100%)
    pallas_call x1, Pallas kernels, local(): pl.pallas_call(gather_and_reduce, out_shape=[pltpu.VMEM((RD, 2 * NB), BF1...  48.1 us
    pallas_call x1, Pallas kernels, local(): pl.pallas_call(apply_shift, out_shape=jax.ShapeDtypeStruct((RD, KD), BF16...  3.05 us

profile of v6, /device:TPU:1, one launch (start us, length us, event | category | flops | bytes accessed | tf_op | source)
XLA Modules:
  0.0 51.1 jit_solution(5037880305099999206)
XLA Ops:
  0.0 48.1 %gather_and_reduce.1 = (bf16[6144,256]{1,0:T(8,128)(2,1)S(1)}, bf16[256,512]{1,0:T(8,128)(2,1)S(1)}, bf16[6144,512]{1,0:T(8,128)(2,1)S(1)}) custom-call(s32[2]{0:T(128)} %offsets.1, bf16[2,8,6144]{2,1,0:T(8,128)(2,1)} %panels.1, bf16[6144,512]{1,0:T(8,128)(2,1)} %eig.1, f32[2,128,128]{2,1,0:T(8,128)} %tf.1), custom_call_target="tpu_custom_call" | custom-call | tf_op jit(solution)/shard_map/gather_and_reduce/pallas_call | solution.py:389
  48.1 3.1 %apply_shift.1 = bf16[6144,512]{1,0:T(8,128)(2,1)} custom-call(bf16[6144,256]{1,0:T(8,128)(2,1)S(1)} %get-tuple-element.8.HT, bf16[256,512]{1,0:T(8,128)(2,1)S(1)} %get-tuple-element.9.Y, bf16[6144,512]{1,0:T(8,128)(2,1)S(1)} %get-tuple-element.10.E), custom_call_target="tpu_custom_call" | custom-call | tf_op jit(solution)/shard_map/apply_shift/pallas_call | solution.py:430
